TPU v7x, 512 devices: a whole 4x8x8 slice. The times are simulated.
512 devices in a mesh: row: 32 (over z, x), col: 16 (over y, core).
Axes of the slice: x: 4, y: 8, z: 8, core: 2. Of those that a mesh axis runs over, the one named last changes fastest.
Arguments:
- activations: bfloat16 [262144, 4096], P(('row', 'col')), may hold values from -110 to 110, as said below
- sketch: bfloat16 [4096, 128], P('col'), may hold values from -0.09375 to 0.09375
Outputs:
- basis: float32 [262144, 128], P(('row', 'col'))
- components: float32 [4096, 128], P('col')
Inputs may be any that keep to these rules, and one draw needn't show every extreme that they name: `activations`: rows and features carry different scales.
All inputs are finite; a program needn't handle non-finite values.
Results may differ from a plain program's by a relative error of at most 0.003.
Values may be sent and summed in bfloat16 or wider, within the bound.
A program may use at most 64 MiB of HBM per device.

v0:
```python
import jax
import jax.numpy as jnp
from jax import lax
from jax.sharding import PartitionSpec as P


def gram_total(block):
    local_gram = lax.dot_general(
        block, block, (((0,), (0,)), ((), ())), precision=lax.Precision.HIGHEST
    )
    return lax.psum(local_gram, ("row", "col"))


def orthonormal(block):
    lower = jnp.linalg.cholesky(gram_total(block))
    return lax.linalg.triangular_solve(lower, block, left_side=False, lower=True, transpose_a=True)


def on_device(activations, sketch):
    rows_total = activations.shape[0] * lax.axis_size("row") * lax.axis_size("col")
    columns = activations
    first = jnp.dot(
        columns,
        lax.all_gather(sketch, "col", axis=0, tiled=True),
        preferred_element_type=jnp.float32,
    )
    ortho_one = orthonormal(first)
    data_wide = activations.astype(jnp.float32)
    local_coeffs = lax.dot_general(
        data_wide, ortho_one, (((0,), (0,)), ((), ())), precision=lax.Precision.HIGHEST
    )
    coeffs = lax.psum(local_coeffs, ("row", "col"))
    second = jnp.dot(data_wide, coeffs, precision=lax.Precision.HIGHEST)
    ortho_two = orthonormal(second)
    scale_root = jnp.sqrt(jnp.float32(rows_total))
    basis = ortho_two * scale_root
    columns = data_wide
    inner = lax.psum_scatter(
        lax.dot_general(
            columns, ortho_two, (((0,), (0,)), ((), ())), precision=lax.Precision.HIGHEST
        ),
        "col",
        scatter_dimension=0,
        tiled=True,
    )
    projected = lax.psum(inner, "row")
    return (basis, projected / scale_root)


def solution(mesh):
    placed = (P(("row", "col"), None), P("col", None))
    return jax.shard_map(
        on_device,
        mesh=mesh,
        in_specs=placed,
        out_specs=(P(("row", "col"), None), P("col", None)),
        check_vma=False,
    )
```

profile of v0, /device:TPU:1, one launch (start us, length us, event | category | flops | bytes accessed | tf_op | source)
XLA Modules:
  0.0 1129.4 jit_solution(16643835548828621495)
XLA Ops:
  7.2 0.0 all-gather.2.cloned.1.call-start
  7.2 0.7 all-gather.2.cloned.1.call-update
  7.9 0.0 all-reduce.5.cloned.1.call-start
  7.9 48.9 %all-gather.2.cloned.1.call-done = bf16[4096,128]{1,0:T(8,128)(2,1)} async-done(((bf16[256,128]{1,0:T(8,128)(2,1)}), bf16[4096,128]{1,0:T(8,128)(2,1)}) %all-gather.2.cloned.1.call-update) | async-done | bytes 1048592 | tf_op jit(solution)/shard_map/all_gather | solution.py:24
  56.9 3.7 fusion.9
  60.6 1.2 fusion.10
  61.8 0.0 all-reduce.5.cloned.1.call-update
  61.8 0.0 all-reduce.7.cloned.1.call-start
  61.9 258.7 %all-reduce.5.cloned.1.call-done = f32[128,128]{0,1:T(8,128)} async-done(((f32[128,128]{0,1:T(8,128)}), f32[128,128]{0,1:T(8,128)}) %all-reduce.5.cloned.1.call-update) | async-done | bytes 65552 | tf_op jit(solution)/shard_map/psum | solution.py:11
  320.6 0.9 copy.5
  321.5 0.9 fusion.6
  322.4 11.7 %cholesky.44 = f32[128,128]{1,0:T(8,128)S(1)} custom-call(f32[128,128]{1,0:T(8,128)S(1)} %fusion.6), custom_call_target="Cholesky" | custom-call | tf_op jit(solution)/shard_map/jit(cholesky)/cholesky | solution.py:15
  334.2 0.6 compare_reduce_fusion.1
  334.8 0.7 fusion.1
  335.5 9.8 custom-call.6
  345.3 0.4 convolution_bitcast_fusion.3
  345.7 5.3 convolution_bitcast_fusion.1
  351.0 0.0 all-reduce.7.cloned.1.call-update
  351.0 0.2 all-reduce.9.cloned.1.call-start
  351.3 271.2 %all-reduce.7.cloned.1.call-done = f32[4096,128]{0,1:T(8,128)} async-done(((f32[4096,128]{0,1:T(8,128)}), f32[4096,128]{0,1:T(8,128)}) %all-reduce.7.cloned.1.call-update) | async-done | bytes 2097168 | tf_op jit(solution)/shard_map/psum | solution.py:32
  622.4 7.0 fusion.11
  629.4 1.0 fusion.12
  630.5 0.0 all-reduce.9.cloned.1.call-update
  630.5 0.0 reduce-scatter.2.cloned.1.call-start
  630.5 255.5 %all-reduce.9.cloned.1.call-done = f32[128,128]{0,1:T(8,128)} async-done(((f32[128,128]{0,1:T(8,128)}), f32[128,128]{0,1:T(8,128)}) %all-reduce.9.cloned.1.call-update) | async-done | bytes 65552 | tf_op jit(solution)/shard_map/psum | solution.py:11
  886.1 0.9 copy.7
  887.0 0.9 fusion.4
  887.8 11.7 %cholesky.55 = f32[128,128]{1,0:T(8,128)S(1)} custom-call(f32[128,128]{1,0:T(8,128)S(1)} %fusion.4), custom_call_target="Cholesky" | custom-call | tf_op jit(solution)/shard_map/jit(cholesky)/cholesky | solution.py:15
  899.6 0.6 compare_reduce_fusion
  900.2 0.7 fusion.2
  900.9 9.8 custom-call.7
  910.7 0.4 broadcast_multiply_fusion
  911.1 5.4 convolution_bitcast_fusion
  916.5 0.0 reduce-scatter.2.cloned.1.call-update
  916.5 0.0 all-reduce.11.cloned.1.call-start
  916.6 51.5 %reduce-scatter.2.cloned.1.call-done = f32[256,128]{0,1:T(8,128)} async-done(((f32[4096,128]{0,1:T(8,128)}), f32[256,128]{0,1:T(8,128)}) %reduce-scatter.2.cloned.1.call-update) | async-done | bytes 131088 | tf_op jit(solution)/shard_map/reduce_scatter | solution.py:38
  968.1 0.0 all-reduce.11.cloned.1.call-update
  968.2 0.8 copy.8
  969.0 151.9 %all-reduce.11.cloned.1.call-done = f32[256,128]{0,1:T(8,128)} async-done(((f32[256,128]{0,1:T(8,128)}), f32[256,128]{0,1:T(8,128)}) %all-reduce.11.cloned.1.call-update) | async-done | bytes 131088 | tf_op jit(solution)/shard_map/psum | solution.py:46
  1120.9 0.9 broadcast_multiply_fusion.1
  1121.8 0.8 copy.9
  (2 shorter events, 0.1 us)
Async XLA Ops:
  7.2 49.7 %all-gather.2.cloned.1.call-start = ((), (), s32[]{:S(2)}) async-start(), calls=%async_computation.1 | async-start | bytes 1114112 | tf_op jit(solution)/shard_map/all_gather | solution.py:24
  7.9 312.7 %all-reduce.5.cloned.1.call-start = ((), (), s32[]{:S(2)}) async-start(), calls=%async_computation.2 | async-start | bytes 131072 | tf_op jit(solution)/shard_map/psum | solution.py:11
  61.8 560.6 %all-reduce.7.cloned.1.call-start = ((), (), s32[]{:S(2)}) async-start(), calls=%async_computation.3 | async-start | bytes 4194304 | tf_op jit(solution)/shard_map/psum | solution.py:32
  351.0 535.0 %all-reduce.9.cloned.1.call-start = ((), (), s32[]{:S(2)}) async-start(), calls=%async_computation.4 | async-start | bytes 131072 | tf_op jit(solution)/shard_map/psum | solution.py:11
  630.5 337.6 %reduce-scatter.2.cloned.1.call-start = ((), (), s32[]{:S(2)}) async-start(), calls=%async_computation.5 | async-start | bytes 2228224 | tf_op jit(solution)/shard_map/reduce_scatter | solution.py:38
  916.5 204.3 %all-reduce.11.cloned.1.call-start = ((), (), s32[]{:S(2)}) async-start(), calls=%async_computation.6 | async-start | bytes 262144 | tf_op jit(solution)/shard_map/psum | solution.py:46
Sparse Core Ops, SparseCore 0:
  10.1 46.6 all-gather.1
  62.4 258.1 all-reduce.4
  351.1 271.2 all-reduce.6
  630.6 255.4 all-reduce.8
  916.6 51.4 reduce-scatter.1
  971.8 148.9 all-reduce.10
where the time goes:
time: 1130 us
  waiting for transfers between devices  1040 us (92%)
  other arithmetic  48.3 us (4%)
  matrix products  24.5 us (2%)
  between operations  14.2 us (1%)
    psum x2, waiting for transfers between devices, gram_total(): return lax.psum(local_gram, ('row', 'col'))  514 us
    psum x1, waiting for transfers between devices, on_device(): coeffs = lax.psum(local_coeffs, ('row', 'col'))  271 us
    psum x1, waiting for transfers between devices, on_device(): projected = lax.psum(inner, 'row')  152 us
    reduce_scatter x1, waiting for transfers between devices, on_device(): lax.psum_scatter(lax.dot_general(columns, ortho_two, (((0,), (0,)), ((),...  51.5 us
    all_gather x1, waiting for transfers between devices, on_device(): lax.all_gather(sketch, 'col', axis=0, tiled=True)  48.9 us
    another operation x6, other arithmetic, orthonormal(): lower = jnp.linalg.cholesky(gram_total(block))  24.8 us
  transfers between devices with their start and end apart: 6, of which 6 were waited for; matrix products, arithmetic and copies ran while one was open for 0% of the time, Pallas kernels for 0%

commit v1 on v0

v1 whole, which is shorter than its diff:
```python
import math

import jax
import jax.numpy as jnp
from jax import lax
from jax.experimental import pallas as pl
from jax.experimental.pallas import tpu as pltpu
from jax.sharding import PartitionSpec as P

f32, bf16 = jnp.float32, jnp.bfloat16
NX, NY, NZ = 4, 8, 8
K, BLOCK, ROWS = 128, 256, 512
NT = (((1,), (1,)), ((), ()))
RING8 = (4, 3, 5, 2, 6, 1, 7)
RING4 = (2, 1, 3)


def split2(value):
    high = value.astype(bf16)
    return high, (value - high.astype(f32)).astype(bf16)


def split3(value):
    high = value.astype(bf16)
    rest = value - high.astype(f32)
    middle = rest.astype(bf16)
    return high, middle, (rest - middle.astype(f32)).astype(bf16)


def times_transposed(left, right):
    lh, ll = split2(left)
    rh, rl = split2(right)
    return lax.dot_general(
        jnp.concatenate([lh, ll, lh], axis=1),
        jnp.concatenate([rh, rh, rl], axis=1),
        NT,
        preferred_element_type=f32,
    )


def cholesky_stage(b, work):
    base = pl.multiple_of(b * 8, 8)
    panel = work[pl.ds(base, 8), :]
    g, w = panel[:, :K], panel[:, K:]
    lane = lax.broadcasted_iota(jnp.int32, (8, K), 1)
    sub = lax.broadcasted_iota(jnp.int32, (8, K), 0)
    pivots = [
        jnp.broadcast_to(jnp.sum(jnp.where(lane == base + k, g, 0.0), axis=1, keepdims=True), (8, K)) for k in range(8)
    ]
    for i in range(8):
        d = jnp.broadcast_to(pivots[i][i : i + 1], (8, K))
        r = lax.rsqrt(d)
        r = r * (1.5 - 0.5 * d * r * r)
        low = jnp.where(sub > i, pivots[i] * r, 0.0)
        keep = sub == i
        gi = jnp.broadcast_to(g[i : i + 1], (8, K)) * r
        wi = jnp.broadcast_to(w[i : i + 1], (8, K)) * r
        g = jnp.where(keep, gi, g - low * gi)
        w = jnp.where(keep, wi, w - low * wi)
        for k in range(i + 1, 8):
            pivots[k] = pivots[k] - low * (jnp.broadcast_to(pivots[k][i : i + 1], (8, K)) * r)
    rows = jnp.concatenate([g, w], axis=1)
    work[pl.ds(base, 8), :] = rows
    left = split3(jnp.where(lane >= base + 8, g, 0.0))
    right = split3(rows)
    pairs = ((0, 0), (0, 1), (1, 0), (1, 1), (0, 2), (2, 0))
    work[...] -= lax.dot_general(
        jnp.concatenate([left[i] for i, _ in pairs], axis=0),
        jnp.concatenate([right[j] for _, j in pairs], axis=0),
        (((0,), (0,)), ((), ())),
        preferred_element_type=f32,
    )


def kernel(
    a_hbm, s_in, sec, w_out, ct_out,
    a_v, s_v, f_acc, ft, work, acc,
    g_local, g_core, g_sum, g_y, g_z, g_x, g_all,
    c_send, c_recv, c_own,
    y1s, z1s, x1s, y1r, z1r, x1r,
    y2s, z2s, x2s, y2r, z2r, x2r,
    y3, z3, x3, f_y, f_z, f_x, e_y, e_z, e_x,
    load_sem, s_send, s_recv, p_recv, send_sems, recv_sems,
):
    row, col = lax.axis_index("row"), lax.axis_index("col")
    z, x, y, h = row // NX, lax.rem(row, NX), col // 2, lax.rem(col, 2)
    other = 1 - h

    def at(zz, xx, yy, hh):
        return (zz * NX + xx, yy * 2 + hh)

    def ring(axis):
        if axis == "y":
            return [(d, lax.rem(y + d, NY), at(z, x, lax.rem(y + d, NY), h)) for d in RING8]
        if axis == "z":
            return [(d, lax.rem(z + d, NZ), at(lax.rem(z + d, NZ), x, y, h)) for d in RING8]
        return [(d, lax.rem(x + d, NX), at(z, lax.rem(x + d, NX), y, h)) for d in RING4]

    partner = at(z, x, y, other)
    pending = []
    slots = {}

    def slot(name):
        return slots.setdefault(name, len(slots))

    def copy_to(name, device, src, dst):
        i = slot(name)
        pltpu.make_async_remote_copy(
            src_ref=src, dst_ref=dst, send_sem=send_sems.at[i], recv_sem=recv_sems.at[i],
            device_id=device, device_id_type=pl.DeviceIdType.MESH,
        ).start()

    def arrived(name, ref):
        pltpu.make_async_copy(ref, ref, recv_sems.at[slot(name)]).wait()
        pending.append((slot(name), ref))

    def scatter(name, axis, src, dst):
        for d, place, device in ring(axis):
            copy_to(name, device, src.at[place], dst.at[d - 1])

    def spread(name, axis, ref):
        for _, _, device in ring(axis):
            copy_to(name, device, ref, ref)

    loads = [
        pltpu.make_async_copy(
            a_hbm.at[:, pl.ds((yy * 2 + hh) * BLOCK, BLOCK)], a_v.at[hh, yy], load_sem.at[0]
        )
        for hh in range(2)
        for yy in range(NY)
    ]
    for load in loads:
        load.start()
    barrier = pltpu.get_barrier_semaphore()
    peers = [partner] + [device for axis in "yzx" for _, _, device in ring(axis)]
    for device in peers:
        pl.semaphore_signal(barrier, inc=1, device_id=device, device_id_type=pl.DeviceIdType.MESH)
    s_v[h, y] = s_in[...]
    pl.semaphore_wait(barrier, len(peers))

    def sketch_copy(src, dst, device, i, recv):
        return pltpu.make_async_remote_copy(
            src_ref=src, dst_ref=dst, send_sem=s_send.at[i], recv_sem=recv.at[i],
            device_id=device, device_id_type=pl.DeviceIdType.MESH,
        )

    mine = s_v.at[h, y]
    for d in (1, 7, 2, 6, 3, 5, 4):
        sketch_copy(mine, mine, at(z, x, lax.rem(y + d, NY), h), d, s_recv).start()

    def hand_on(d, place):
        block = s_v.at[h, place]
        pltpu.make_async_remote_copy(
            src_ref=block, dst_ref=block, send_sem=s_send.at[8 + d], recv_sem=p_recv.at[d],
            device_id=partner, device_id_type=pl.DeviceIdType.MESH,
        ).start()

    def distance(i):
        half = (i + 1) // 2
        return jnp.where(lax.rem(i, 2) == 1, half, lax.rem(NY - half, NY))

    hand_on(0, y)
    pltpu.make_async_copy(a_v, a_v, load_sem.at[0]).wait()
    f_acc[...] = jnp.dot(a_v[h, y], s_v[h, y], preferred_element_type=f32)

    @pl.loop(1, NY)
    def _(i):
        d = distance(i)
        place = lax.rem(y + NY - d, NY)
        block = s_v.at[h, place]
        pltpu.make_async_copy(block, block, s_recv.at[d]).wait()
        hand_on(d, place)
        f_acc[...] += jnp.dot(a_v[h, place], block[...], preferred_element_type=f32)

    @pl.loop(0, NY)
    def _(i):
        d = distance(i)
        place = lax.rem(y + NY - d, NY)
        block = s_v.at[other, place]
        pltpu.make_async_copy(block, block, p_recv.at[d]).wait()
        f_acc[...] += jnp.dot(a_v[other, place], block[...], preferred_element_type=f32)

    def project(p, tall):
        high, low = split2(tall.T)
        ft[:K, :] = high
        ft[K:, :] = low
        both = ft[...]
        square = lax.dot_general(both, both, NT, preferred_element_type=f32)
        gram = (square[:K, :K] + square[K:, K:]) + (square[:K, K:] + square[K:, :K])
        g_local[p] = gram.reshape(2, 8, 8, K)
        copy_to(f"gc{p}", partner, g_local.at[p, other], g_core.at[p])

        @pl.loop(0, NY)
        def _(i):
            both = jnp.dot(ft[...], a_v[other, i], preferred_element_type=f32)
            c_send[p, i] = (both[:K] + both[K:]).astype(bf16)
            copy_to(f"c{p}", partner, c_send.at[p, i], c_recv.at[p, i])

        @pl.loop(0, NY)
        def _(i):
            both = jnp.dot(ft[...], a_v[h, i], preferred_element_type=f32)
            c_own[i] = both[:K] + both[K:]

    def gram_y(p):
        arrived(f"gc{p}", g_core.at[p])
        g_sum[p] = g_local[p, h] + g_core[p]
        scatter(f"gy{p}", "y", g_sum.at[p], g_y.at[p])

    def gram_z(p):
        arrived(f"gy{p}", g_y.at[p])
        g_z[p, z] = g_sum[p, y] + jnp.sum(g_y[p], axis=0)
        spread(f"gz{p}", "z", g_z.at[p, z])

    def gram_x(p):
        arrived(f"gz{p}", g_z.at[p, pl.ds(0, NZ - 1)])
        g_x[p, x] = jnp.sum(g_z[p], axis=0)
        spread(f"gx{p}", "x", g_x.at[p, x])

    def gram_back_y(p):
        arrived(f"gx{p}", g_x.at[p, pl.ds(0, NX - 1)])
        g_all[p, h, y] = jnp.sum(g_x[p], axis=0)
        spread(f"ga{p}", "y", g_all.at[p, h, y])

    def gram_back_core(p):
        arrived(f"ga{p}", g_all.at[p, h, pl.ds(0, NY - 1)])
        copy_to(f"gb{p}", partner, g_all.at[p, h], g_all.at[p, h])

    def gram_done(p):
        arrived(f"gb{p}", g_all.at[p, other])
        ri = lax.broadcasted_iota(jnp.int32, (K, K), 0)
        ci = lax.broadcasted_iota(jnp.int32, (K, K), 1)
        work[:, :K] = g_all[p].reshape(K, K)
        work[:, K:] = jnp.where(ri == ci, 1.0, 0.0)

    def stages(lo, hi):
        @pl.loop(lo, hi)
        def _(b):
            cholesky_stage(b, work)

    def one(p):
        arrived(f"c{p}", c_recv.at[p])

        @pl.loop(0, NY // 2)
        def _(j):
            even = c_own[2 * j] + c_recv[p, 2 * j].astype(f32)
            odd = c_own[2 * j + 1] + c_recv[p, 2 * j + 1].astype(f32)
            for place, value in ((2 * j, even), (2 * j + 1, odd)):
                y1s[p, place] = value[:32].astype(bf16)
                for q in range(NX):
                    x1s[p, q, place] = value[64 + 16 * q : 80 + 16 * q].astype(bf16)
            for q in range(NZ):
                r, c = 32 + 8 * (q // 2), K * (q % 2)
                tiles = [value[r : r + 8, c : c + K] for value in (even, odd)]
                z1s[p, q, pl.ds(pl.multiple_of(j * 16, 16), 16)] = jnp.concatenate(tiles, axis=0).astype(bf16)

        scatter(f"y1{p}", "y", y1s.at[p], y1r.at[p])
        scatter(f"z1{p}", "z", z1s.at[p], z1r.at[p])
        scatter(f"x1{p}", "x", x1s.at[p], x1r.at[p])

    def total(own, parts):
        return own.astype(f32) + jnp.sum(parts.astype(f32), axis=0)

    def two(p):
        arrived(f"y1{p}", y1r.at[p])
        value = total(y1s[p, y], y1r[p])
        for q in range(NZ):
            y2s[p, q] = value[8 * (q // 2) : 8 * (q // 2) + 8, K * (q % 2) : K * (q % 2) + K]
        scatter(f"y2{p}", "z", y2s.at[p], y2r.at[p])
        arrived(f"z1{p}", z1r.at[p])
        z2s[p] = total(z1s[p, z], z1r[p]).reshape(NY, 8, K)
        scatter(f"z2{p}", "y", z2s.at[p], z2r.at[p])
        arrived(f"x1{p}", x1r.at[p])
        x2s[p] = total(x1s[p, x], x1r[p])
        scatter(f"x2{p}", "y", x2s.at[p], x2r.at[p])

    def three(p):
        arrived(f"y2{p}", y2r.at[p])
        y3[p, x] = total(y2s[p, z], y2r[p])
        spread(f"y3{p}", "x", y3.at[p, x])
        arrived(f"z2{p}", z2r.at[p])
        z3[p, x] = total(z2s[p, y], z2r[p])
        spread(f"z3{p}", "x", z3.at[p, x])
        arrived(f"x2{p}", x2r.at[p])
        x3[p, z] = total(x2s[p, y], x2r[p])
        spread(f"x3{p}", "z", x3.at[p, z])

    def sums(p):
        arrived(f"y3{p}", y3.at[p, pl.ds(0, NX - 1)])
        yield jnp.sum(y3[p], axis=0)
        arrived(f"z3{p}", z3.at[p, pl.ds(0, NX - 1)])
        yield jnp.sum(z3[p], axis=0)
        arrived(f"x3{p}", x3.at[p, pl.ds(0, NZ - 1)])
        yield jnp.sum(x3[p], axis=0)

    project(0, f_acc[...])
    gram_y(0)
    one(0)
    gram_z(0)
    two(0)
    gram_x(0)
    three(0)
    gram_back_y(0)
    gather = sums(0)
    f_y[h, y, z] = next(gather)
    spread("y4", "z", f_y.at[h, y, z])
    f_z[h, z, y] = next(gather)
    spread("z4", "y", f_z.at[h, z, y])
    f_x[h, x, y] = next(gather)
    spread("x4", "y", f_x.at[h, x, y])
    next(gather, None)
    gram_back_core(0)
    arrived("y4", f_y.at[h, y, pl.ds(0, NZ - 1)])
    spread("y5", "y", f_y.at[h, y])
    arrived("z4", f_z.at[h, z, pl.ds(0, NY - 1)])
    spread("z5", "z", f_z.at[h, z])
    arrived("x4", f_x.at[h, x, pl.ds(0, NY - 1)])
    spread("x5", "x", f_x.at[h, x])
    gram_done(0)
    stages(0, 16)
    arrived("y5", f_y.at[h, pl.ds(0, NY - 1)])
    copy_to("y6", partner, f_y.at[h], f_y.at[h])
    arrived("z5", f_z.at[h, pl.ds(0, NZ - 1)])
    copy_to("z6", partner, f_z.at[h], f_z.at[h])
    arrived("x5", f_x.at[h, pl.ds(0, NX - 1)])
    copy_to("x6", partner, f_x.at[h], f_x.at[h])

    def tiles(ref):
        rows = [jnp.concatenate([ref[2 * k], ref[2 * k + 1]], axis=1) for k in range(4)]
        return jnp.concatenate(rows, axis=0)

    def second_part(half):
        @pl.loop(0, NY)
        def _(i):
            parts = [tiles(f_y.at[half, i])]
            parts += [tiles(f_z.at[half, :, i])]
            parts += [f_x[half, q, i] for q in range(NX)]
            high, low = split2(jnp.concatenate(parts, axis=0))
            acc[...] += lax.dot_general(
                a_v[half, i], jnp.concatenate([high, low], axis=0), NT, preferred_element_type=f32
            )

    acc[...] = jnp.zeros_like(acc)
    second_part(h)
    arrived("y6", f_y.at[other])
    arrived("z6", f_z.at[other])
    arrived("x6", f_x.at[other])
    second_part(other)
    sec[...] = times_transposed(acc[:, :K] + acc[:, K:], work[:, K:])

    project(1, sec[...])
    gram_y(1)
    one(1)
    gram_z(1)
    two(1)
    gram_x(1)
    three(1)
    gram_back_y(1)
    gather = sums(1)
    e_y[z] = next(gather)
    spread("y7", "z", e_y.at[z])
    e_z[z] = next(gather)
    spread("z7", "z", e_z.at[z])
    e_x[x] = next(gather)
    spread("x7", "x", e_x.at[x])
    next(gather, None)
    gram_back_core(1)
    gram_done(1)
    stages(0, 16)
    w_out[...] = work[:, K:]
    arrived("y7", e_y.at[pl.ds(0, NZ - 1)])
    arrived("z7", e_z.at[pl.ds(0, NZ - 1)])
    arrived("x7", e_x.at[pl.ds(0, NX - 1)])
    ct_out[...] = jnp.concatenate([tiles(e_y), tiles(e_z)] + [e_x[q] for q in range(NX)], axis=0)

    for i, ref in pending:
        pltpu.make_async_copy(ref, ref, send_sems.at[i]).wait()
    for i in range(1, NY):
        pltpu.make_async_copy(mine, mine, s_send.at[i]).wait()
    for i in range(NY):
        pltpu.make_async_copy(mine, mine, s_send.at[8 + i]).wait()


def finish(scale_root, sec, w, ct, basis, components):
    basis[...] = times_transposed(sec[...], w[...]) * scale_root
    components[...] = times_transposed(ct[...].T, w[...]) / scale_root


def on_device(activations, sketch):
    rows_total = activations.shape[0] * lax.axis_size("row") * lax.axis_size("col")
    vmem = pltpu.VMEM
    shapes = [
        vmem((2, NY, ROWS, BLOCK), bf16), vmem((2, NY, BLOCK, K), bf16), vmem((ROWS, K), f32),
        vmem((2 * K, ROWS), bf16), vmem((K, 2 * K), f32), vmem((ROWS, 2 * K), f32),
        vmem((2, 2, 8, 8, K), f32), vmem((2, 8, 8, K), f32), vmem((2, 8, 8, K), f32), vmem((2, NY - 1, 8, K), f32),
        vmem((2, NZ, 8, K), f32), vmem((2, NX, 8, K), f32), vmem((2, 2, 8, 8, K), f32),
        vmem((2, NY, K, BLOCK), bf16), vmem((2, NY, K, BLOCK), bf16), vmem((NY, K, BLOCK), f32),
        vmem((2, NY, 32, BLOCK), bf16), vmem((2, NZ, 64, K), bf16), vmem((2, NX, NY, 16, BLOCK), bf16),
        vmem((2, NY - 1, 32, BLOCK), bf16), vmem((2, NZ - 1, 64, K), bf16), vmem((2, NX - 1, NY, 16, BLOCK), bf16),
        vmem((2, NZ, 8, K), f32), vmem((2, NY, 8, K), f32), vmem((2, NY, 16, BLOCK), f32),
        vmem((2, NZ - 1, 8, K), f32), vmem((2, NY - 1, 8, K), f32), vmem((2, NY - 1, 16, BLOCK), f32),
        vmem((2, NX, 8, K), f32), vmem((2, NX, 8, K), f32), vmem((2, NZ, 16, BLOCK), f32),
        vmem((2, NY, NZ, 8, K), f32), vmem((2, NZ, NY, 8, K), f32), vmem((2, NX, NY, 16, BLOCK), f32),
        vmem((NZ, 8, K), f32), vmem((NZ, 8, K), f32), vmem((NX, 16, BLOCK), f32),
        pltpu.SemaphoreType.DMA((1,)), pltpu.SemaphoreType.DMA((16,)), pltpu.SemaphoreType.DMA((8,)),
        pltpu.SemaphoreType.DMA((8,)), pltpu.SemaphoreType.DMA((48,)), pltpu.SemaphoreType.DMA((48,)),
    ]
    here = pl.BlockSpec(memory_space=pltpu.VMEM)
    sec, w, ct = pl.pallas_call(
        kernel,
        out_shape=(
            jax.ShapeDtypeStruct((ROWS, K), f32),
            jax.ShapeDtypeStruct((K, K), f32),
            jax.ShapeDtypeStruct((K, BLOCK), f32),
        ),
        in_specs=[pl.BlockSpec(memory_space=pl.ANY), here],
        out_specs=(here, here, here),
        scratch_shapes=shapes,
        compiler_params=pltpu.CompilerParams(
            collective_id=0, has_side_effects=True, vmem_limit_bytes=48 << 20
        ),
        name="subspace",
    )(activations, sketch)

    def last(*refs):
        finish(math.sqrt(rows_total), *refs)

    return pl.pallas_call(
        last,
        out_shape=(jax.ShapeDtypeStruct((ROWS, K), f32), jax.ShapeDtypeStruct((BLOCK, K), f32)),
        in_specs=[here, here, here],
        out_specs=(here, here),
        name="outputs",
    )(sec, w, ct)


def solution(mesh):
    placed = (P(("row", "col"), None), P("col", None))
    return jax.shard_map(
        on_device,
        mesh=mesh,
        in_specs=placed,
        out_specs=(P(("row", "col"), None), P("col", None)),
        check_vma=False,
    )
```

time: 1130 us -> 108 us (0.10)
  waiting for transfers between devices: 1040 us -> 0 us
  Pallas kernels: 0 us -> 103 us
  other arithmetic: 48.3 us -> 0 us
  matrix products: 24.5 us -> 0 us
  between operations: 14.2 us -> 0.66 us
    psum x4 -> x0, waiting for transfers between devices: 937 us -> none  [the longest x2 514 us: gram_total(): return lax.psum(local_gram, ('row', 'col'))]
    pallas_call x0 -> x2, Pallas kernels: none -> 103 us  [the longest x1 101 us: on_device(): pl.pallas_call(kernel, out_shape=(jax.ShapeDtypeStruct((ROWS, K), f32), j...]
    reduce_scatter x1 -> x0, waiting for transfers between devices: 51.5 us -> none  [on_device(): lax.psum_scatter(lax.dot_general(columns, ortho_two, (((0,), (0,)), ((),...]
    all_gather x1 -> x0, waiting for transfers between devices: 48.9 us -> none  [on_device(): lax.all_gather(sketch, 'col', axis=0, tiled=True)]
    another operation x10 -> x0, other arithmetic: 45.7 us -> none  [the longest x6 24.8 us: orthonormal(): lower = jnp.linalg.cholesky(gram_total(block))]
    dot_general x6 -> x0, matrix products: 23.6 us -> none  [the longest x1 7.02 us: on_device(): second = jnp.dot(data_wide, coeffs, precision=lax.Precision.HIGHEST)]
  transfers between devices with their start and end apart: 6 -> 0, of which waited for: 6 -> 0; matrix products, arithmetic and copies ran while one was open for 0% -> 0% of each run, Pallas kernels for 0% -> 0%
where the time goes in v1:
time: 108 us
  Pallas kernels  103 us (95%)
  local copies, waits for them, and re-layouts  4.97 us (5%)
    pallas_call x1, Pallas kernels, on_device(): pl.pallas_call(kernel, out_shape=(jax.ShapeDtypeStruct((ROWS, K), f32), j...  101 us
    unnamed x10, local copies, waits for them, and re-layouts  4.97 us

profile of v1, /device:TPU:1, one launch (start us, length us, event | category | flops | bytes accessed | tf_op | source)
XLA Modules:
  0.0 108.2 jit_solution(9699776310839276165)
XLA Ops:
  0.6 0.0 copy-start
  0.6 2.2 %copy-done = bf16[512,4096]{1,0:T(8,128)(2,1)S(1)} copy-done((bf16[512,4096]{1,0:T(8,128)(2,1)S(1)}, bf16[512,4096]{1,0:T(8,128)(2,1)}, u32[]{:S(2)}) %copy-start) | copy-done | bytes 4194328
  2.8 0.0 copy-start.3
  2.8 0.8 copy-done.3
  3.7 100.5 %subspace.1 = (f32[512,128]{1,0:T(8,128)S(1)}, f32[128,128]{1,0:T(8,128)S(1)}, f32[128,256]{1,0:T(8,128)S(1)}) custom-call(bf16[512,4096]{1,0:T(8,128)(2,1)S(1)} %copy-done, bf16[256,128]{1,0:T(8,128)(2,1)S(1)} %copy-done.3), custom_call_target="tpu_custom_call" | custom-call | tf_op jit(solution)/shard_map/subspace/pallas_call | solution.py:408
  104.2 0.0 copy-start.1
  104.2 0.7 copy-done.1
  104.9 0.0 copy-start.2
  104.9 0.6 copy-done.2
  105.5 0.0 copy-start.4
  105.5 0.6 copy-done.4
  106.1 2.1 %outputs.1 = (f32[512,128]{1,0:T(8,128)}, f32[256,128]{1,0:T(8,128)}) custom-call(f32[512,128]{1,0:T(8,128)} %copy-done.1, f32[128,128]{1,0:T(8,128)} %copy-done.4, f32[128,256]{1,0:T(8,128)} %copy-done.2), custom_call_target="tpu_custom_call" | custom-call | tf_op jit(solution)/shard_map/outputs/pallas_call | solution.py:427
Async XLA Ops:
  0.6 2.2 %copy-start = (bf16[512,4096]{1,0:T(8,128)(2,1)S(1)}, bf16[512,4096]{1,0:T(8,128)(2,1)}, u32[]{:S(2)}) copy-start(bf16[512,4096]{1,0:T(8,128)(2,1)} %a_hbm.1) | copy-start | bytes 12582916
  2.8 0.8 copy-start.3
  104.2 0.7 copy-start.1
  104.9 0.6 copy-start.2
  105.5 0.6 copy-start.4

commit v2 on v1

v2 whole, which is shorter than its diff:
```python
import functools
import math

import jax
import jax.numpy as jnp
from jax import lax
from jax.experimental import pallas as pl
from jax.experimental.pallas import tpu as pltpu
from jax.sharding import PartitionSpec as P

f32, bf16 = jnp.float32, jnp.bfloat16
NX, NY, NZ = 4, 8, 8
K, BLOCK, ROWS = 128, 256, 512
PIVOTS = 16
QUARTER = BLOCK // NX
NT = (((1,), (1,)), ((), ()))
RING8 = (4, 3, 5, 2, 6, 1, 7)
RING4 = (2, 1, 3)
NEAR, FAR = (1, 7, 2, 6), (4, 3, 5)
COL16 = (8, 7, 9, 6, 10, 5, 11, 4, 12, 3, 13, 2, 14, 1, 15)


def split2(value):
    high = value.astype(bf16)
    return high, (value - high.astype(f32)).astype(bf16)


def split3(value):
    high = value.astype(bf16)
    rest = value - high.astype(f32)
    middle = rest.astype(bf16)
    return high, middle, (rest - middle.astype(f32)).astype(bf16)


def times_transposed(left, right):
    lh, ll = split2(left)
    rh, rl = split2(right)
    return lax.dot_general(
        jnp.concatenate([lh, ll, lh], axis=1),
        jnp.concatenate([rh, rh, rl], axis=1),
        NT,
        preferred_element_type=f32,
    )


def cholesky_stage(b, work):
    base = pl.multiple_of(b * PIVOTS, PIVOTS)
    panel = work[pl.ds(base, PIVOTS), :]
    g, w = panel[:, :K], panel[:, K:]
    shape = (PIVOTS, K)
    lane = lax.broadcasted_iota(jnp.int32, shape, 1)
    sub = lax.broadcasted_iota(jnp.int32, shape, 0)

    def column(k):
        return jnp.broadcast_to(jnp.sum(jnp.where(lane == base + k, g, 0.0), axis=1, keepdims=True), shape)

    def row(value, i):
        return jnp.broadcast_to(value[i : i + 1], shape)

    pivots = [column(k) for k in range(PIVOTS)]
    for i in range(PIVOTS):
        r = lax.rsqrt(row(pivots[i], i))
        low = jnp.where(sub > i, pivots[i] * r, 0.0)
        gi, wi = row(g, i) * r, row(w, i) * r
        g = jnp.where(sub == i, gi, g - low * gi)
        w = jnp.where(sub == i, wi, w - low * wi)
        for k in range(i + 1, PIVOTS):
            pivots[k] = pivots[k] - low * (row(pivots[k], i) * r)
    rows = jnp.concatenate([g, w], axis=1)
    work[pl.ds(base, PIVOTS), :] = rows
    left = split3(jnp.where(lane >= base + PIVOTS, g, 0.0))
    right = split3(rows)
    pairs = ((0, 0), (0, 1), (1, 0), (1, 1), (0, 2), (2, 0))
    work[...] -= lax.dot_general(
        jnp.concatenate([left[i] for i, _ in pairs], axis=0),
        jnp.concatenate([right[j] for _, j in pairs], axis=0),
        (((0,), (0,)), ((), ())),
        preferred_element_type=f32,
    )


def kernel(
    scale_root, a_hbm, s_hbm, basis, components,
    sec, a_v, s_v, f_acc, ft, work, acc,
    g_local, g_col, g_z, g_x, g_all,
    c_send, c_recv,
    y1s, z1s, x1s, y1r, z1r, x1r,
    y2s, z2s, x2s, y2r, z2r, x2r,
    y3, z3, x3, f_y, f_z, f_x, e_y, e_z, e_x,
    load_sem, s_send, s_recv, p_recv, q_send, q_recv, c_sems, f_sems, send_sems, recv_sems,
):
    row, col = lax.axis_index("row"), lax.axis_index("col")
    z, x, y, h = row // NX, lax.rem(row, NX), col // 2, lax.rem(col, 2)
    other = 1 - h

    def at(zz, xx, yy, hh):
        return (zz * NX + xx, yy * 2 + hh)

    def ring(axis):
        if axis == "y":
            return [(d, lax.rem(y + d, NY), at(z, x, lax.rem(y + d, NY), h)) for d in RING8]
        if axis == "col":
            spots = [lax.rem(col + d, 2 * NY) for d in COL16]
            return [(d, c, (row, c)) for d, c in zip(COL16, spots)]
        if axis == "z":
            return [(d, lax.rem(z + d, NZ), at(lax.rem(z + d, NZ), x, y, h)) for d in RING8]
        return [(d, lax.rem(x + d, NX), at(z, lax.rem(x + d, NX), y, h)) for d in RING4]

    partner = at(z, x, y, other)
    pending = []
    slots = {}

    def slot(name):
        return slots.setdefault(name, len(slots))

    def copy_to(name, device, src, dst):
        i = slot(name)
        pltpu.make_async_remote_copy(
            src_ref=src, dst_ref=dst, send_sem=send_sems.at[i], recv_sem=recv_sems.at[i],
            device_id=device, device_id_type=pl.DeviceIdType.MESH,
        ).start()

    def arrived(name, ref):
        pltpu.make_async_copy(ref, ref, recv_sems.at[slot(name)]).wait()
        pending.append((slot(name), ref))

    def scatter(name, axis, src, dst):
        for d, place, device in ring(axis):
            copy_to(name, device, src.at[place], dst.at[d - 1])

    def spread(name, axis, ref):
        for _, _, device in ring(axis):
            copy_to(name, device, ref, ref)

    loads = [
        pltpu.make_async_copy(
            a_hbm.at[:, pl.ds((yy * 2 + hh) * BLOCK, BLOCK)], a_v.at[hh, yy], load_sem.at[0]
        )
        for hh in range(2)
        for yy in range(NY)
    ]
    own_sketch = pltpu.make_async_copy(s_hbm, s_v.at[h, y], load_sem.at[1])
    own_sketch.start()
    for load in loads:
        load.start()
    barrier = pltpu.get_barrier_semaphore()
    peers = [device for axis in ("col", "z", "x") for _, _, device in ring(axis)]
    for device in peers:
        pl.semaphore_signal(barrier, inc=1, device_id=device, device_id_type=pl.DeviceIdType.MESH)
    own_sketch.wait()
    pl.semaphore_wait(barrier, len(peers))

    def sketch_copy(block, device, sends, recvs, d):
        return pltpu.make_async_remote_copy(
            src_ref=block, dst_ref=block, send_sem=sends, recv_sem=recvs.at[d],
            device_id=device, device_id_type=pl.DeviceIdType.MESH,
        )

    mine = s_v.at[h, y]
    span = pl.ds(pl.multiple_of(x * QUARTER, QUARTER), QUARTER)
    for d in FAR:
        sketch_copy(s_v.at[h, y, span], at(z, x, lax.rem(y + d, NY), h), s_send.at[d], q_recv, d).start()
    for d in NEAR:
        sketch_copy(mine, at(z, x, lax.rem(y + d, NY), h), s_send.at[d], s_recv, d).start()

    def hand_on(d, place):
        sketch_copy(s_v.at[h, place], partner, s_send.at[8 + d], p_recv, d).start()

    def distance(i):
        half = (i + 1) // 2
        return jnp.where(lax.rem(i, 2) == 1, half, lax.rem(NY - half, NY))

    def come(lo, hi, size):
        @pl.loop(lo, hi)
        def _(i):
            d = distance(i)
            place = lax.rem(y + NY - d, NY)
            block = s_v.at[h, place]
            part = s_v.at[h, place, pl.ds(0, size)]
            pltpu.make_async_copy(part, part, s_recv.at[d]).wait()
            hand_on(d, place)
            f_acc[...] += jnp.dot(a_v[h, place], block[...], preferred_element_type=f32)

    hand_on(0, y)
    pltpu.make_async_copy(a_v, a_v, load_sem.at[0]).wait()
    f_acc[...] = jnp.dot(a_v[h, y], s_v[h, y], preferred_element_type=f32)
    come(1, 3, BLOCK)
    for d in FAR:
        quarter = s_v.at[h, lax.rem(y + NY - d, NY), span]
        pltpu.make_async_copy(quarter, quarter, q_recv.at[d]).wait()
        for _, _, device in ring("x"):
            sketch_copy(quarter, device, q_send.at[d], s_recv, d).start()
    come(3, 5, BLOCK)
    come(5, 8, BLOCK - QUARTER)

    @pl.loop(0, NY)
    def _(i):
        d = distance(i)
        place = lax.rem(y + NY - d, NY)
        block = s_v.at[other, place]
        pltpu.make_async_copy(block, block, p_recv.at[d]).wait()
        f_acc[...] += jnp.dot(a_v[other, place], block[...], preferred_element_type=f32)

    def project(p, tall):
        high, low = split2(tall.T)
        ft[:K, :] = high
        ft[K:, :] = low
        both = ft[...]
        square = lax.dot_general(both, both, NT, preferred_element_type=f32)
        gram = (square[:K, :K] + square[K:, K:]) + (square[:K, K:] + square[K:, :K])
        g_local[p] = gram.reshape(2 * NY, 8, K)
        scatter(f"gc{p}", "col", g_local.at[p], g_col.at[p])

        @pl.loop(0, NY // 2)
        def _(j):
            for i in (2 * j, 2 * j + 1):
                both = jnp.dot(ft[...], a_v[other, i], preferred_element_type=f32)
                c_send[p, i] = (both[:K] + both[K:]).astype(bf16)
            pair = pl.ds(2 * j, 2)
            pltpu.make_async_remote_copy(
                src_ref=c_send.at[p, pair], dst_ref=c_recv.at[p, pair],
                send_sem=c_sems.at[p, 0, j], recv_sem=c_sems.at[p, 1, j],
                device_id=partner, device_id_type=pl.DeviceIdType.MESH,
            ).start()

        @pl.loop(0, NY // 2)
        def _(j):
            values = []
            for i in (2 * j, 2 * j + 1):
                both = jnp.dot(ft[...], a_v[h, i], preferred_element_type=f32)
                values.append(both[:K] + both[K:])
            pair = c_recv.at[p, pl.ds(2 * j, 2)]
            pltpu.make_async_copy(pair, pair, c_sems.at[p, 1, j]).wait()
            values = [value + pair[i].astype(f32) for i, value in enumerate(values)]
            for place, value in zip((2 * j, 2 * j + 1), values):
                y1s[p, place] = value[:32].astype(bf16)
                for q in range(NX):
                    x1s[p, q, place] = value[64 + 16 * q : 80 + 16 * q].astype(bf16)
            for q in range(NZ):
                r, c = 32 + 8 * (q // 2), K * (q % 2)
                both = jnp.concatenate([value[r : r + 8, c : c + K] for value in values], axis=0)
                z1s[p, q, pl.ds(pl.multiple_of(j * 16, 16), 16)] = both.astype(bf16)

        scatter(f"x1{p}", "x", x1s.at[p], x1r.at[p])
        scatter(f"y1{p}", "y", y1s.at[p], y1r.at[p])
        scatter(f"z1{p}", "z", z1s.at[p], z1r.at[p])

    def gram_z(p):
        arrived(f"gc{p}", g_col.at[p])
        g_z[p, z] = g_local[p, col] + jnp.sum(g_col[p], axis=0)
        spread(f"gz{p}", "z", g_z.at[p, z])

    def gram_x(p):
        arrived(f"gz{p}", g_z.at[p, pl.ds(0, NZ - 1)])
        g_x[p, x] = jnp.sum(g_z[p], axis=0)
        spread(f"gx{p}", "x", g_x.at[p, x])

    def gram_back(p):
        arrived(f"gx{p}", g_x.at[p, pl.ds(0, NX - 1)])
        g_all[p, col] = jnp.sum(g_x[p], axis=0)
        spread(f"ga{p}", "col", g_all.at[p, col])

    def gram_done(p):
        arrived(f"ga{p}", g_all.at[p, pl.ds(0, 2 * NY - 1)])
        ri = lax.broadcasted_iota(jnp.int32, (K, K), 0)
        ci = lax.broadcasted_iota(jnp.int32, (K, K), 1)
        work[:, :K] = g_all[p].reshape(K, K)
        work[:, K:] = jnp.where(ri == ci, 1.0, 0.0)

    def stages(lo, hi):
        @pl.loop(lo, hi)
        def _(b):
            cholesky_stage(b, work)

    def total(own, parts):
        return own.astype(f32) + jnp.sum(parts.astype(f32), axis=0)

    def two(p):
        arrived(f"x1{p}", x1r.at[p])
        x2s[p] = total(x1s[p, x], x1r[p]).astype(bf16)
        scatter(f"x2{p}", "y", x2s.at[p], x2r.at[p])
        arrived(f"y1{p}", y1r.at[p])
        value = total(y1s[p, y], y1r[p])
        for q in range(NZ):
            y2s[p, q] = value[8 * (q // 2) : 8 * (q // 2) + 8, K * (q % 2) : K * (q % 2) + K]
        scatter(f"y2{p}", "z", y2s.at[p], y2r.at[p])
        arrived(f"z1{p}", z1r.at[p])
        z2s[p] = total(z1s[p, z], z1r[p]).reshape(NY, 8, K)
        scatter(f"z2{p}", "y", z2s.at[p], z2r.at[p])

    def three(p):
        arrived(f"y2{p}", y2r.at[p])
        y3[p, x] = total(y2s[p, z], y2r[p])
        spread(f"y3{p}", "x", y3.at[p, x])
        arrived(f"z2{p}", z2r.at[p])
        z3[p, x] = total(z2s[p, y], z2r[p])
        spread(f"z3{p}", "x", z3.at[p, x])
        arrived(f"x2{p}", x2r.at[p])
        x3[p, z] = total(x2s[p, y], x2r[p])
        spread(f"x3{p}", "z", x3.at[p, z])

    def sums(p):
        arrived(f"y3{p}", y3.at[p, pl.ds(0, NX - 1)])
        yield jnp.sum(y3[p], axis=0)
        arrived(f"z3{p}", z3.at[p, pl.ds(0, NX - 1)])
        yield jnp.sum(z3[p], axis=0)
        arrived(f"x3{p}", x3.at[p, pl.ds(0, NZ - 1)])
        yield jnp.sum(x3[p], axis=0)

    project(0, f_acc[...])
    gram_z(0)
    gram_x(0)
    two(0)
    gram_back(0)
    three(0)
    gather = sums(0)
    f_y[h, y, z] = next(gather)
    spread("y4", "z", f_y.at[h, y, z])
    f_z[h, z, y] = next(gather)
    spread("z4", "y", f_z.at[h, z, y])
    f_x[h, x, y] = next(gather)
    spread("x4", "y", f_x.at[h, x, y])
    gram_done(0)
    arrived("y4", f_y.at[h, y, pl.ds(0, NZ - 1)])
    arrived("z4", f_z.at[h, z, pl.ds(0, NY - 1)])
    arrived("x4", f_x.at[h, x, pl.ds(0, NY - 1)])

    def fanned(i, block, device):
        pltpu.make_async_remote_copy(
            src_ref=block, dst_ref=block, send_sem=f_sems.at[0, i], recv_sem=f_sems.at[1, i],
            device_id=device, device_id_type=pl.DeviceIdType.MESH,
        ).start()

    for k, (d, _, device) in enumerate(ring("y")):
        fanned(d, f_y.at[h, y], device)
        fanned(8 + d, f_z.at[h, z], ring("z")[k][2])
        if k < NX - 1:
            d, _, device = ring("x")[k]
            fanned(16 + d, f_x.at[h, x], device)
    copy_to("y6", partner, f_y.at[h, y], f_y.at[h, y])
    copy_to("z6", partner, f_z.at[h, z], f_z.at[h, z])
    copy_to("x6", partner, f_x.at[h, x], f_x.at[h, x])
    stages(0, K // PIVOTS)

    def fan_in(name, i, block):
        pltpu.make_async_copy(block, block, f_sems.at[1, i]).wait()
        copy_to(name, partner, block, block)

    for d in (1, 7, 2, 6, 3, 5, 4):
        fan_in("y6", d, f_y.at[h, lax.rem(y + NY - d, NY)])
        fan_in("z6", 8 + d, f_z.at[h, lax.rem(z + NZ - d, NZ)])
        if d in (7, 2, 6):
            e = {7: 1, 2: 3, 6: 2}[d]
            fan_in("x6", 16 + e, f_x.at[h, lax.rem(x + NX - e, NX)])

    def tiles(ref):
        rows = [jnp.concatenate([ref[2 * k], ref[2 * k + 1]], axis=1) for k in range(4)]
        return jnp.concatenate(rows, axis=0)

    def second_part(half):
        @pl.loop(0, NY)
        def _(i):
            parts = [tiles(f_y.at[half, i])]
            parts += [tiles(f_z.at[half, :, i])]
            parts += [f_x[half, q, i] for q in range(NX)]
            high, low = split2(jnp.concatenate(parts, axis=0))
            acc[...] += lax.dot_general(
                a_v[half, i], jnp.concatenate([high, low], axis=0), NT, preferred_element_type=f32
            )

    acc[...] = jnp.zeros_like(acc)
    second_part(h)
    arrived("y6", f_y.at[other])
    arrived("z6", f_z.at[other])
    arrived("x6", f_x.at[other])
    second_part(other)
    sec[...] = times_transposed(acc[:, :K] + acc[:, K:], work[:, K:])

    project(1, sec[...])
    gram_z(1)
    gram_x(1)
    two(1)
    gram_back(1)
    three(1)
    gram_done(1)
    stages(0, 2)
    gather = sums(1)
    e_y[z] = next(gather)
    spread("y7", "z", e_y.at[z])
    e_z[z] = next(gather)
    spread("z7", "z", e_z.at[z])
    e_x[x] = next(gather)
    spread("x7", "x", e_x.at[x])
    stages(2, K // PIVOTS)
    inverse = work[:, K:]
    basis[...] = times_transposed(sec[...], inverse) * scale_root
    arrived("y7", e_y.at[pl.ds(0, NZ - 1)])
    arrived("z7", e_z.at[pl.ds(0, NZ - 1)])
    arrived("x7", e_x.at[pl.ds(0, NX - 1)])
    summed = jnp.concatenate([tiles(e_y), tiles(e_z)] + [e_x[q] for q in range(NX)], axis=0)
    components[...] = times_transposed(summed.T, inverse) / scale_root

    for i, ref in pending:
        pltpu.make_async_copy(ref, ref, send_sems.at[i]).wait()
    for d in range(NY):
        pltpu.make_async_copy(mine, mine, s_send.at[8 + d]).wait()
    for d in NEAR:
        pltpu.make_async_copy(mine, mine, s_send.at[d]).wait()
    for d in FAR:
        quarter = s_v.at[h, y, pl.ds(0, QUARTER)]
        pltpu.make_async_copy(quarter, quarter, s_send.at[d]).wait()
        three_quarters = s_v.at[h, y, pl.ds(0, BLOCK - QUARTER)]
        pltpu.make_async_copy(three_quarters, three_quarters, q_send.at[d]).wait()
    for p in range(2):
        for j in range(NY // 2):
            pair = c_send.at[p, pl.ds(0, 2)]
            pltpu.make_async_copy(pair, pair, c_sems.at[p, 0, j]).wait()
    for d in range(1, NY):
        pltpu.make_async_copy(f_y.at[h, y], f_y.at[h, y], f_sems.at[0, d]).wait()
        pltpu.make_async_copy(f_z.at[h, z], f_z.at[h, z], f_sems.at[0, 8 + d]).wait()
    for d in range(1, NX):
        pltpu.make_async_copy(f_x.at[h, x], f_x.at[h, x], f_sems.at[0, 16 + d]).wait()


def on_device(activations, sketch):
    rows_total = activations.shape[0] * lax.axis_size("row") * lax.axis_size("col")
    vmem = pltpu.VMEM
    shapes = [
        vmem((ROWS, K), f32), vmem((2, NY, ROWS, BLOCK), bf16), vmem((2, NY, BLOCK, K), bf16), vmem((ROWS, K), f32),
        vmem((2 * K, ROWS), bf16), vmem((K, 2 * K), f32), vmem((ROWS, 2 * K), f32),
        vmem((2, 2 * NY, 8, K), f32), vmem((2, 2 * NY - 1, 8, K), f32),
        vmem((2, NZ, 8, K), f32), vmem((2, NX, 8, K), f32), vmem((2, 2 * NY, 8, K), f32),
        vmem((2, NY, K, BLOCK), bf16), vmem((2, NY, K, BLOCK), bf16),
        vmem((2, NY, 32, BLOCK), bf16), vmem((2, NZ, 64, K), bf16), vmem((2, NX, NY, 16, BLOCK), bf16),
        vmem((2, NY - 1, 32, BLOCK), bf16), vmem((2, NZ - 1, 64, K), bf16), vmem((2, NX - 1, NY, 16, BLOCK), bf16),
        vmem((2, NZ, 8, K), f32), vmem((2, NY, 8, K), f32), vmem((2, NY, 16, BLOCK), bf16),
        vmem((2, NZ - 1, 8, K), f32), vmem((2, NY - 1, 8, K), f32), vmem((2, NY - 1, 16, BLOCK), bf16),
        vmem((2, NX, 8, K), f32), vmem((2, NX, 8, K), f32), vmem((2, NZ, 16, BLOCK), f32),
        vmem((2, NY, NZ, 8, K), f32), vmem((2, NZ, NY, 8, K), f32), vmem((2, NX, NY, 16, BLOCK), f32),
        vmem((NZ, 8, K), f32), vmem((NZ, 8, K), f32), vmem((NX, 16, BLOCK), f32),
        pltpu.SemaphoreType.DMA((2,)), pltpu.SemaphoreType.DMA((16,)), pltpu.SemaphoreType.DMA((8,)),
        pltpu.SemaphoreType.DMA((8,)), pltpu.SemaphoreType.DMA((8,)), pltpu.SemaphoreType.DMA((8,)),
        pltpu.SemaphoreType.DMA((2, 2, NY // 2)), pltpu.SemaphoreType.DMA((2, 24)),
        pltpu.SemaphoreType.DMA((48,)), pltpu.SemaphoreType.DMA((48,)),
    ]
    here = pl.BlockSpec(memory_space=pltpu.VMEM)
    far = pl.BlockSpec(memory_space=pltpu.HBM)
    return pl.pallas_call(
        functools.partial(kernel, math.sqrt(rows_total)),
        out_shape=(jax.ShapeDtypeStruct((ROWS, K), f32), jax.ShapeDtypeStruct((BLOCK, K), f32)),
        in_specs=[far, far],
        out_specs=(here, here),
        scratch_shapes=shapes,
        compiler_params=pltpu.CompilerParams(
            collective_id=0, has_side_effects=True, vmem_limit_bytes=48 << 20
        ),
        name="subspace",
    )(activations, sketch)


def solution(mesh):
    placed = (P(("row", "col"), None), P("col", None))
    return jax.shard_map(
        on_device,
        mesh=mesh,
        in_specs=placed,
        out_specs=(P(("row", "col"), None), P("col", None)),
        check_vma=False,
    )
```

time: 108 us -> 97.5 us (0.903)
  Pallas kernels: 103 us -> 92.3 us
    pallas_call x2 -> x1, Pallas kernels: 103 us -> 92.3 us  [on_device(): pl.pallas_call(functools.partial(kernel, math.sqrt(rows_total)), out_shap...]
    unnamed x10 -> x6, local copies, waits for them, and re-layouts: 4.97 us -> 4.38 us
where the time goes in v2:
time: 97.5 us; the launch traced here: 97.3 us
  Pallas kernels  92.3 us (95%)
  local copies, waits for them, and re-layouts  4.38 us (4%)
    pallas_call x1, Pallas kernels, on_device(): pl.pallas_call(functools.partial(kernel, math.sqrt(rows_total)), out_shap...  92.3 us
    unnamed x6, local copies, waits for them, and re-layouts  4.38 us

profile of v2, /device:TPU:1, one launch (start us, length us, event | category | flops | bytes accessed | tf_op | source)
XLA Modules:
  0.0 97.3 jit_solution(7573199530098819118)
XLA Ops:
  0.6 0.0 copy-start
  0.6 2.2 %copy-done = bf16[512,4096]{1,0:T(8,128)(2,1)S(1)} copy-done((bf16[512,4096]{1,0:T(8,128)(2,1)S(1)}, bf16[512,4096]{1,0:T(8,128)(2,1)}, u32[]{:S(2)}) %copy-start) | copy-done | bytes 4194328
  2.8 0.0 copy-start.1
  2.8 0.8 copy-done.1
  3.7 92.3 %subspace.1 = (f32[512,128]{1,0:T(8,128)S(1)}, f32[256,128]{1,0:T(8,128)S(1)}) custom-call(bf16[512,4096]{1,0:T(8,128)(2,1)S(1)} %copy-done, bf16[256,128]{1,0:T(8,128)(2,1)S(1)} %copy-done.1), custom_call_target="tpu_custom_call" | custom-call | tf_op jit(solution)/shard_map/subspace/pallas_call | solution.py:448
  95.9 0.7 copy.6
  96.7 0.7 copy.7
Async XLA Ops:
  0.6 2.2 %copy-start = (bf16[512,4096]{1,0:T(8,128)(2,1)S(1)}, bf16[512,4096]{1,0:T(8,128)(2,1)}, u32[]{:S(2)}) copy-start(bf16[512,4096]{1,0:T(8,128)(2,1)} %a_hbm.1) | copy-start | bytes 12582916
  2.8 0.8 copy-start.1

commit v3 on v2

--- a/solution.py
+++ b/solution.py
@@ -81,12 +81,12 @@
 
 def kernel(
     scale_root, a_hbm, s_hbm, basis, components,
-    sec, a_v, s_v, f_acc, ft, work, acc,
+    sec, a_v, s_v, f_acc, ft, work, coeffs,
     g_local, g_col, g_z, g_x, g_all,
     c_send, c_recv,
     y1s, z1s, x1s, y1r, z1r, x1r,
-    y2s, z2s, x2s, y2r, z2r, x2r,
-    y3, z3, x3, f_y, f_z, f_x, e_y, e_z, e_x,
+    y2s, z2s, x2s, v2s, w2s, y2r, z2r, x2r, v2r, w2r,
+    y3, z3, x3, v3, w3, f_y, f_z, f_x, e_y, e_z, e_x,
     load_sem, s_send, s_recv, p_recv, q_send, q_recv, c_sems, f_sems, send_sems, recv_sems,
 ):
     row, col = lax.axis_index("row"), lax.axis_index("col")
@@ -107,6 +107,10 @@
         return [(d, lax.rem(x + d, NX), at(z, lax.rem(x + d, NX), y, h)) for d in RING4]
 
     partner = at(z, x, y, other)
+
+    def columns(half, place):
+        return a_v[half, :, pl.ds(pl.multiple_of(place * BLOCK, BLOCK), BLOCK)]
+
     pending = []
     slots = {}
 
@@ -134,7 +138,7 @@
 
     loads = [
         pltpu.make_async_copy(
-            a_hbm.at[:, pl.ds((yy * 2 + hh) * BLOCK, BLOCK)], a_v.at[hh, yy], load_sem.at[0]
+            a_hbm.at[:, pl.ds((yy * 2 + hh) * BLOCK, BLOCK)], a_v.at[hh, :, pl.ds(yy * BLOCK, BLOCK)], load_sem.at[0]
         )
         for hh in range(2)
         for yy in range(NY)
@@ -166,55 +170,60 @@
     def hand_on(d, place):
         sketch_copy(s_v.at[h, place], partner, s_send.at[8 + d], p_recv, d).start()
 
-    def distance(i):
-        half = (i + 1) // 2
-        return jnp.where(lax.rem(i, 2) == 1, half, lax.rem(NY - half, NY))
-
-    def come(lo, hi, size):
-        @pl.loop(lo, hi)
-        def _(i):
-            d = distance(i)
-            place = lax.rem(y + NY - d, NY)
-            block = s_v.at[h, place]
-            part = s_v.at[h, place, pl.ds(0, size)]
+    def origin(d):
+        return lax.rem(y + NY - d, NY)
+
+    def come(ds, size):
+        for d in ds:
+            part = s_v.at[h, origin(d), pl.ds(0, size)]
             pltpu.make_async_copy(part, part, s_recv.at[d]).wait()
-            hand_on(d, place)
-            f_acc[...] += jnp.dot(a_v[h, place], block[...], preferred_element_type=f32)
+            hand_on(d, origin(d))
+
+    def add(half, ds):
+        blocks = [(half, origin(d)) for d in ds]
+        f_acc[...] += sum(jnp.dot(columns(*b), s_v[b], preferred_element_type=f32) for b in blocks)
+
+    def add_other(ds):
+        for d in ds:
+            block = s_v.at[other, origin(d)]
+            pltpu.make_async_copy(block, block, p_recv.at[d]).wait()
+        add(other, ds)
 
     hand_on(0, y)
     pltpu.make_async_copy(a_v, a_v, load_sem.at[0]).wait()
-    f_acc[...] = jnp.dot(a_v[h, y], s_v[h, y], preferred_element_type=f32)
-    come(1, 3, BLOCK)
+    f_acc[...] = jnp.dot(columns(h, y), s_v[h, y], preferred_element_type=f32)
+    come(NEAR[:2], BLOCK)
     for d in FAR:
-        quarter = s_v.at[h, lax.rem(y + NY - d, NY), span]
+        quarter = s_v.at[h, origin(d), span]
         pltpu.make_async_copy(quarter, quarter, q_recv.at[d]).wait()
         for _, _, device in ring("x"):
             sketch_copy(quarter, device, q_send.at[d], s_recv, d).start()
-    come(3, 5, BLOCK)
-    come(5, 8, BLOCK - QUARTER)
-
-    @pl.loop(0, NY)
-    def _(i):
-        d = distance(i)
-        place = lax.rem(y + NY - d, NY)
-        block = s_v.at[other, place]
-        pltpu.make_async_copy(block, block, p_recv.at[d]).wait()
-        f_acc[...] += jnp.dot(a_v[other, place], block[...], preferred_element_type=f32)
+    come(NEAR[2:], BLOCK)
+    add(h, NEAR)
+    add_other((0,) + NEAR)
+    come(FAR, BLOCK - QUARTER)
+    add(h, FAR)
+    add_other(FAR)
 
     def project(p, tall):
         high, low = split2(tall.T)
         ft[:K, :] = high
         ft[K:, :] = low
-        both = ft[...]
-        square = lax.dot_general(both, both, NT, preferred_element_type=f32)
-        gram = (square[:K, :K] + square[K:, K:]) + (square[:K, K:] + square[K:, :K])
-        g_local[p] = gram.reshape(2 * NY, 8, K)
-        scatter(f"gc{p}", "col", g_local.at[p], g_col.at[p])
+
+        def gram_first():
+            both = ft[...]
+            square = lax.dot_general(both, both, NT, preferred_element_type=f32)
+            gram = (square[:K, :K] + square[K:, K:]) + (square[:K, K:] + square[K:, :K])
+            g_local[p] = gram.reshape(2 * NY, 8, K)
+            scatter(f"gc{p}", "col", g_local.at[p], g_col.at[p])
+
+        if p == 1:
+            gram_first()
 
         @pl.loop(0, NY // 2)
         def _(j):
             for i in (2 * j, 2 * j + 1):
-                both = jnp.dot(ft[...], a_v[other, i], preferred_element_type=f32)
+                both = jnp.dot(ft[...], columns(other, i), preferred_element_type=f32)
                 c_send[p, i] = (both[:K] + both[K:]).astype(bf16)
             pair = pl.ds(2 * j, 2)
             pltpu.make_async_remote_copy(
@@ -223,11 +232,14 @@
                 device_id=partner, device_id_type=pl.DeviceIdType.MESH,
             ).start()
 
+        if p == 0:
+            gram_first()
+
         @pl.loop(0, NY // 2)
         def _(j):
             values = []
             for i in (2 * j, 2 * j + 1):
-                both = jnp.dot(ft[...], a_v[h, i], preferred_element_type=f32)
+                both = jnp.dot(ft[...], columns(h, i), preferred_element_type=f32)
                 values.append(both[:K] + both[K:])
             pair = c_recv.at[p, pl.ds(2 * j, 2)]
             pltpu.make_async_copy(pair, pair, c_sems.at[p, 1, j]).wait()
@@ -235,7 +247,8 @@
             for place, value in zip((2 * j, 2 * j + 1), values):
                 y1s[p, place] = value[:32].astype(bf16)
                 for q in range(NX):
-                    x1s[p, q, place] = value[64 + 16 * q : 80 + 16 * q].astype(bf16)
+                    both = [value[r + 8 * q : r + 8 * q + 8] for r in (64, 96)]
+                    x1s[p, q, place] = jnp.concatenate(both, axis=0).astype(bf16)
             for q in range(NZ):
                 r, c = 32 + 8 * (q // 2), K * (q % 2)
                 both = jnp.concatenate([value[r : r + 8, c : c + K] for value in values], axis=0)
@@ -277,8 +290,15 @@
 
     def two(p):
         arrived(f"x1{p}", x1r.at[p])
-        x2s[p] = total(x1s[p, x], x1r[p]).astype(bf16)
-        scatter(f"x2{p}", "y", x2s.at[p], x2r.at[p])
+        value = total(x1s[p, x], x1r[p])
+        if p == 0:
+            v2s[...] = value[:, :8]
+            scatter("v2", "y", v2s, v2r)
+            w2s[...] = value[:, 8:]
+            scatter("w2", "z", w2s, w2r)
+        else:
+            x2s[...] = value.astype(bf16)
+            scatter("x2", "y", x2s, x2r)
         arrived(f"y1{p}", y1r.at[p])
         value = total(y1s[p, y], y1r[p])
         for q in range(NZ):
@@ -295,35 +315,47 @@
         arrived(f"z2{p}", z2r.at[p])
         z3[p, x] = total(z2s[p, y], z2r[p])
         spread(f"z3{p}", "x", z3.at[p, x])
-        arrived(f"x2{p}", x2r.at[p])
-        x3[p, z] = total(x2s[p, y], x2r[p])
-        spread(f"x3{p}", "z", x3.at[p, z])
+        if p == 0:
+            arrived("v2", v2r)
+            v3[z] = total(v2s[y], v2r[...])
+            spread("v3", "z", v3.at[z])
+            arrived("w2", w2r)
+            w3[y] = total(w2s[z], w2r[...])
+            spread("w3", "y", w3.at[y])
+        else:
+            arrived("x2", x2r)
+            x3[z] = total(x2s[y], x2r[...])
+            spread("x3", "z", x3.at[z])
 
     def sums(p):
         arrived(f"y3{p}", y3.at[p, pl.ds(0, NX - 1)])
         yield jnp.sum(y3[p], axis=0)
         arrived(f"z3{p}", z3.at[p, pl.ds(0, NX - 1)])
         yield jnp.sum(z3[p], axis=0)
-        arrived(f"x3{p}", x3.at[p, pl.ds(0, NZ - 1)])
-        yield jnp.sum(x3[p], axis=0)
+        for name, ref in (("v3", v3), ("w3", w3)) if p == 0 else (("x3", x3),):
+            arrived(name, ref.at[pl.ds(0, NZ - 1)])
+            yield jnp.sum(ref[...], axis=0)
 
     project(0, f_acc[...])
     gram_z(0)
+    two(0)
     gram_x(0)
-    two(0)
+    three(0)
     gram_back(0)
-    three(0)
     gather = sums(0)
     f_y[h, y, z] = next(gather)
     spread("y4", "z", f_y.at[h, y, z])
     f_z[h, z, y] = next(gather)
     spread("z4", "y", f_z.at[h, z, y])
-    f_x[h, x, y] = next(gather)
-    spread("x4", "y", f_x.at[h, x, y])
+    f_x[h, x, 0, y] = next(gather)
+    spread("v4", "y", f_x.at[h, x, 0, y])
+    f_x[h, x, 1, z] = next(gather)
+    spread("w4", "z", f_x.at[h, x, 1, z])
     gram_done(0)
     arrived("y4", f_y.at[h, y, pl.ds(0, NZ - 1)])
     arrived("z4", f_z.at[h, z, pl.ds(0, NY - 1)])
-    arrived("x4", f_x.at[h, x, pl.ds(0, NY - 1)])
+    arrived("v4", f_x.at[h, x, 0, pl.ds(0, NY - 1)])
+    arrived("w4", f_x.at[h, x, 1, pl.ds(0, NZ - 1)])
 
     def fanned(i, block, device):
         pltpu.make_async_remote_copy(
@@ -360,21 +392,20 @@
     def second_part(half):
         @pl.loop(0, NY)
         def _(i):
-            parts = [tiles(f_y.at[half, i])]
-            parts += [tiles(f_z.at[half, :, i])]
-            parts += [f_x[half, q, i] for q in range(NX)]
+            parts = [tiles(f_y.at[half, i]), tiles(f_z.at[half, :, i])]
+            parts += [f_x[half, q, k, i] for k in range(2) for q in range(NX)]
             high, low = split2(jnp.concatenate(parts, axis=0))
-            acc[...] += lax.dot_general(
-                a_v[half, i], jnp.concatenate([high, low], axis=0), NT, preferred_element_type=f32
-            )
-
-    acc[...] = jnp.zeros_like(acc)
-    second_part(h)
+            span = pl.ds(pl.multiple_of(i * BLOCK, BLOCK), BLOCK)
+            coeffs[half, :, span] = jnp.concatenate([high, low], axis=0)
+
+        both = lax.dot_general(a_v[half], coeffs[half], NT, preferred_element_type=f32)
+        return both[:, :K] + both[:, K:]
+
+    f_acc[...] = second_part(h)
     arrived("y6", f_y.at[other])
     arrived("z6", f_z.at[other])
     arrived("x6", f_x.at[other])
-    second_part(other)
-    sec[...] = times_transposed(acc[:, :K] + acc[:, K:], work[:, K:])
+    sec[...] = times_transposed(f_acc[...] + second_part(other), work[:, K:])
 
     project(1, sec[...])
     gram_z(1)
@@ -397,7 +428,7 @@
     arrived("y7", e_y.at[pl.ds(0, NZ - 1)])
     arrived("z7", e_z.at[pl.ds(0, NZ - 1)])
     arrived("x7", e_x.at[pl.ds(0, NX - 1)])
-    summed = jnp.concatenate([tiles(e_y), tiles(e_z)] + [e_x[q] for q in range(NX)], axis=0)
+    summed = jnp.concatenate([tiles(e_y), tiles(e_z)] + [e_x[q, k : k + 8] for k in (0, 8) for q in range(NX)], axis=0)
     components[...] = times_transposed(summed.T, inverse) / scale_root
 
     for i, ref in pending:
@@ -426,17 +457,20 @@
     rows_total = activations.shape[0] * lax.axis_size("row") * lax.axis_size("col")
     vmem = pltpu.VMEM
     shapes = [
-        vmem((ROWS, K), f32), vmem((2, NY, ROWS, BLOCK), bf16), vmem((2, NY, BLOCK, K), bf16), vmem((ROWS, K), f32),
-        vmem((2 * K, ROWS), bf16), vmem((K, 2 * K), f32), vmem((ROWS, 2 * K), f32),
+        vmem((ROWS, K), f32), vmem((2, ROWS, NY * BLOCK), bf16), vmem((2, NY, BLOCK, K), bf16), vmem((ROWS, K), f32),
+        vmem((2 * K, ROWS), bf16), vmem((K, 2 * K), f32), vmem((2, 2 * K, NY * BLOCK), bf16),
         vmem((2, 2 * NY, 8, K), f32), vmem((2, 2 * NY - 1, 8, K), f32),
         vmem((2, NZ, 8, K), f32), vmem((2, NX, 8, K), f32), vmem((2, 2 * NY, 8, K), f32),
         vmem((2, NY, K, BLOCK), bf16), vmem((2, NY, K, BLOCK), bf16),
         vmem((2, NY, 32, BLOCK), bf16), vmem((2, NZ, 64, K), bf16), vmem((2, NX, NY, 16, BLOCK), bf16),
         vmem((2, NY - 1, 32, BLOCK), bf16), vmem((2, NZ - 1, 64, K), bf16), vmem((2, NX - 1, NY, 16, BLOCK), bf16),
-        vmem((2, NZ, 8, K), f32), vmem((2, NY, 8, K), f32), vmem((2, NY, 16, BLOCK), bf16),
-        vmem((2, NZ - 1, 8, K), f32), vmem((2, NY - 1, 8, K), f32), vmem((2, NY - 1, 16, BLOCK), bf16),
-        vmem((2, NX, 8, K), f32), vmem((2, NX, 8, K), f32), vmem((2, NZ, 16, BLOCK), f32),
-        vmem((2, NY, NZ, 8, K), f32), vmem((2, NZ, NY, 8, K), f32), vmem((2, NX, NY, 16, BLOCK), f32),
+        vmem((2, NZ, 8, K), f32), vmem((2, NY, 8, K), f32), vmem((NY, 16, BLOCK), bf16),
+        vmem((NY, 8, BLOCK), f32), vmem((NZ, 8, BLOCK), f32),
+        vmem((2, NZ - 1, 8, K), f32), vmem((2, NY - 1, 8, K), f32), vmem((NY - 1, 16, BLOCK), bf16),
+        vmem((NY - 1, 8, BLOCK), f32), vmem((NZ - 1, 8, BLOCK), f32),
+        vmem((2, NX, 8, K), f32), vmem((2, NX, 8, K), f32), vmem((NZ, 16, BLOCK), f32),
+        vmem((NZ, 8, BLOCK), f32), vmem((NY, 8, BLOCK), f32),
+        vmem((2, NY, NZ, 8, K), f32), vmem((2, NZ, NY, 8, K), f32), vmem((2, NX, 2, NY, 8, BLOCK), f32),
         vmem((NZ, 8, K), f32), vmem((NZ, 8, K), f32), vmem((NX, 16, BLOCK), f32),
         pltpu.SemaphoreType.DMA((2,)), pltpu.SemaphoreType.DMA((16,)), pltpu.SemaphoreType.DMA((8,)),
         pltpu.SemaphoreType.DMA((8,)), pltpu.SemaphoreType.DMA((8,)), pltpu.SemaphoreType.DMA((8,)),
@@ -452,7 +486,7 @@
         out_specs=(here, here),
         scratch_shapes=shapes,
         compiler_params=pltpu.CompilerParams(
-            collective_id=0, has_side_effects=True, vmem_limit_bytes=48 << 20
+            collective_id=0, has_side_effects=True, vmem_limit_bytes=52 << 20
         ),
         name="subspace",
     )(activations, sketch)

time: 97.5 us -> 90 us (0.923)
  Pallas kernels: 92.3 us -> 87 us
  local copies, waits for them, and re-layouts: 4.38 us -> 2.19 us
    pallas_call x1, Pallas kernels: 92.3 us -> 87 us  [on_device(): pl.pallas_call(functools.partial(kernel, math.sqrt(rows_total)), out_shap...]
    unnamed x6 -> x4, local copies, waits for them, and re-layouts: 4.38 us -> 2.19 us
where the time goes in v3:
time: 90 us; the launch traced here: 89.9 us
  Pallas kernels  87 us (97%)
  local copies, waits for them, and re-layouts  2.19 us (2%)
    pallas_call x1, Pallas kernels, on_device(): pl.pallas_call(functools.partial(kernel, math.sqrt(rows_total)), out_shap...  87 us
    unnamed x4, local copies, waits for them, and re-layouts  2.19 us

profile of v3, /device:TPU:1, one launch (start us, length us, event | category | flops | bytes accessed | tf_op | source)
XLA Modules:
  0.0 89.9 jit_solution(7235383575789591220)
XLA Ops:
  0.6 0.0 copy-start
  0.6 0.8 copy-done
  1.5 87.0 %subspace.1 = (f32[512,128]{1,0:T(8,128)S(1)}, f32[256,128]{1,0:T(8,128)S(1)}) custom-call(bf16[512,4096]{1,0:T(8,128)(2,1)} %a_hbm.1, bf16[256,128]{1,0:T(8,128)(2,1)S(1)} %copy-done), custom_call_target="tpu_custom_call" | custom-call | tf_op jit(solution)/shard_map/subspace/pallas_call | solution.py:482
  88.5 0.7 copy.6
  89.2 0.7 copy.7
Async XLA Ops:
  0.6 0.8 copy-start

commit v4 on v3

--- a/solution.py
+++ b/solution.py
@@ -85,8 +85,8 @@
     g_local, g_col, g_z, g_x, g_all,
     c_send, c_recv,
     y1s, z1s, x1s, y1r, z1r, x1r,
-    y2s, z2s, x2s, v2s, w2s, y2r, z2r, x2r, v2r, w2r,
-    y3, z3, x3, v3, w3, f_y, f_z, f_x, e_y, e_z, e_x,
+    over_y, over_z, over_y_in, over_z_in, y2s, z2s, x2s, y2r, z2r, x2r,
+    yz3, v3, w3, y_full, z_full, y3, z3, x3, f_y, f_z, f_x, e_y, e_z, e_x,
     load_sem, s_send, s_recv, p_recv, q_send, q_recv, c_sems, f_sems, send_sems, recv_sems,
 ):
     row, col = lax.axis_index("row"), lax.axis_index("col")
@@ -231,9 +231,6 @@
                 send_sem=c_sems.at[p, 0, j], recv_sem=c_sems.at[p, 1, j],
                 device_id=partner, device_id_type=pl.DeviceIdType.MESH,
             ).start()
-
-        if p == 0:
-            gram_first()
 
         @pl.loop(0, NY // 2)
         def _(j):
@@ -257,6 +254,8 @@
         scatter(f"x1{p}", "x", x1s.at[p], x1r.at[p])
         scatter(f"y1{p}", "y", y1s.at[p], y1r.at[p])
         scatter(f"z1{p}", "z", z1s.at[p], z1r.at[p])
+        if p == 0:
+            gram_first()
 
     def gram_z(p):
         arrived(f"gc{p}", g_col.at[p])
@@ -288,74 +287,85 @@
     def total(own, parts):
         return own.astype(f32) + jnp.sum(parts.astype(f32), axis=0)
 
-    def two(p):
-        arrived(f"x1{p}", x1r.at[p])
-        value = total(x1s[p, x], x1r[p])
-        if p == 0:
-            v2s[...] = value[:, :8]
-            scatter("v2", "y", v2s, v2r)
-            w2s[...] = value[:, 8:]
-            scatter("w2", "z", w2s, w2r)
-        else:
-            x2s[...] = value.astype(bf16)
-            scatter("x2", "y", x2s, x2r)
+    def y_tiles(p):
         arrived(f"y1{p}", y1r.at[p])
         value = total(y1s[p, y], y1r[p])
-        for q in range(NZ):
-            y2s[p, q] = value[8 * (q // 2) : 8 * (q // 2) + 8, K * (q % 2) : K * (q % 2) + K]
-        scatter(f"y2{p}", "z", y2s.at[p], y2r.at[p])
+        return [value[8 * (q // 2) : 8 * (q // 2) + 8, K * (q % 2) : K * (q % 2) + K] for q in range(NZ)]
+
+    def z_tiles(p):
         arrived(f"z1{p}", z1r.at[p])
-        z2s[p] = total(z1s[p, z], z1r[p]).reshape(NY, 8, K)
-        scatter(f"z2{p}", "y", z2s.at[p], z2r.at[p])
-
-    def three(p):
-        arrived(f"y2{p}", y2r.at[p])
-        y3[p, x] = total(y2s[p, z], y2r[p])
-        spread(f"y3{p}", "x", y3.at[p, x])
-        arrived(f"z2{p}", z2r.at[p])
-        z3[p, x] = total(z2s[p, y], z2r[p])
-        spread(f"z3{p}", "x", z3.at[p, x])
-        if p == 0:
-            arrived("v2", v2r)
-            v3[z] = total(v2s[y], v2r[...])
-            spread("v3", "z", v3.at[z])
-            arrived("w2", w2r)
-            w3[y] = total(w2s[z], w2r[...])
-            spread("w3", "y", w3.at[y])
-        else:
-            arrived("x2", x2r)
-            x3[z] = total(x2s[y], x2r[...])
-            spread("x3", "z", x3.at[z])
-
-    def sums(p):
-        arrived(f"y3{p}", y3.at[p, pl.ds(0, NX - 1)])
-        yield jnp.sum(y3[p], axis=0)
-        arrived(f"z3{p}", z3.at[p, pl.ds(0, NX - 1)])
-        yield jnp.sum(z3[p], axis=0)
-        for name, ref in (("v3", v3), ("w3", w3)) if p == 0 else (("x3", x3),):
-            arrived(name, ref.at[pl.ds(0, NZ - 1)])
-            yield jnp.sum(ref[...], axis=0)
+        return total(z1s[p, z], z1r[p]).reshape(NY, 8, K)
+
+    def two_first():
+        arrived("x10", x1r.at[0])
+        value = total(x1s[0, x], x1r[0])
+        for q, tile in enumerate(y_tiles(0)):
+            over_z[q, :, :K] = tile
+            over_z[q, :, K:] = value[q, 8:]
+        scatter("wz", "z", over_z, over_z_in)
+        over_y[:, :, :K] = z_tiles(0)
+        over_y[:, :, K:] = value[:, :8]
+        scatter("wy", "y", over_y, over_y_in)
+
+    def three_first():
+        arrived("wz", over_z_in)
+        value = total(over_z[z], over_z_in[...])
+        yz3[x, :, :K] = value[:, :K]
+        w3[y] = value[:, K:]
+        spread("w3", "y", w3.at[y])
+        arrived("wy", over_y_in)
+        value = total(over_y[y], over_y_in[...])
+        yz3[x, :, K:] = value[:, :K]
+        v3[z] = value[:, K:]
+        spread("v3", "z", v3.at[z])
+        spread("yz3", "x", yz3.at[x])
+
+    def four_first():
+        arrived("yz3", yz3.at[pl.ds(0, NX - 1)])
+        value = jnp.sum(yz3[...], axis=0)
+        arrived("w3", w3.at[pl.ds(0, NY - 1)])
+        z_full[z, :, :K] = value[:, :K]
+        z_full[z, :, K:] = jnp.sum(w3[...], axis=0)
+        spread("z4", "z", z_full.at[z])
+        arrived("v3", v3.at[pl.ds(0, NZ - 1)])
+        y_full[y, :, :K] = value[:, K:]
+        y_full[y, :, K:] = jnp.sum(v3[...], axis=0)
+        spread("y4", "y", y_full.at[y])
+
+    def two():
+        arrived("x11", x1r.at[1])
+        x2s[...] = total(x1s[1, x], x1r[1]).astype(bf16)
+        scatter("x2", "y", x2s, x2r)
+        for q, tile in enumerate(y_tiles(1)):
+            y2s[q] = tile
+        scatter("y2", "z", y2s, y2r)
+        z2s[...] = z_tiles(1)
+        scatter("z2", "y", z2s, z2r)
+
+    def three():
+        arrived("y2", y2r)
+        y3[x] = total(y2s[z], y2r[...])
+        spread("y3", "x", y3.at[x])
+        arrived("z2", z2r)
+        z3[x] = total(z2s[y], z2r[...])
+        spread("z3", "x", z3.at[x])
+        arrived("x2", x2r)
+        x3[z] = total(x2s[y], x2r[...])
+        spread("x3", "z", x3.at[z])
 
     project(0, f_acc[...])
     gram_z(0)
-    two(0)
+    two_first()
     gram_x(0)
-    three(0)
+    three_first()
     gram_back(0)
-    gather = sums(0)
-    f_y[h, y, z] = next(gather)
-    spread("y4", "z", f_y.at[h, y, z])
-    f_z[h, z, y] = next(gather)
-    spread("z4", "y", f_z.at[h, z, y])
-    f_x[h, x, 0, y] = next(gather)
-    spread("v4", "y", f_x.at[h, x, 0, y])
-    f_x[h, x, 1, z] = next(gather)
-    spread("w4", "z", f_x.at[h, x, 1, z])
-    gram_done(0)
-    arrived("y4", f_y.at[h, y, pl.ds(0, NZ - 1)])
-    arrived("z4", f_z.at[h, z, pl.ds(0, NY - 1)])
-    arrived("v4", f_x.at[h, x, 0, pl.ds(0, NY - 1)])
-    arrived("w4", f_x.at[h, x, 1, pl.ds(0, NZ - 1)])
+    four_first()
+    arrived("z4", z_full.at[pl.ds(0, NZ - 1)])
+    f_y[h, y] = z_full[:, :, :K]
+    f_x[h, x, 1] = z_full[:, :, K:]
+    arrived("y4", y_full.at[pl.ds(0, NY - 1)])
+    f_z[h, z] = y_full[:, :, :K]
+    f_x[h, x, 0] = y_full[:, :, K:]
 
     def fanned(i, block, device):
         pltpu.make_async_remote_copy(
@@ -372,6 +382,7 @@
     copy_to("y6", partner, f_y.at[h, y], f_y.at[h, y])
     copy_to("z6", partner, f_z.at[h, z], f_z.at[h, z])
     copy_to("x6", partner, f_x.at[h, x], f_x.at[h, x])
+    gram_done(0)
     stages(0, K // PIVOTS)
 
     def fan_in(name, i, block):
@@ -410,19 +421,21 @@
     project(1, sec[...])
     gram_z(1)
     gram_x(1)
-    two(1)
+    two()
     gram_back(1)
-    three(1)
+    three()
+    arrived("y3", y3.at[pl.ds(0, NX - 1)])
+    e_y[z] = jnp.sum(y3[...], axis=0)
+    spread("y7", "z", e_y.at[z])
+    arrived("z3", z3.at[pl.ds(0, NX - 1)])
+    e_z[z] = jnp.sum(z3[...], axis=0)
+    spread("z7", "z", e_z.at[z])
     gram_done(1)
-    stages(0, 2)
-    gather = sums(1)
-    e_y[z] = next(gather)
-    spread("y7", "z", e_y.at[z])
-    e_z[z] = next(gather)
-    spread("z7", "z", e_z.at[z])
-    e_x[x] = next(gather)
+    stages(0, 3)
+    arrived("x3", x3.at[pl.ds(0, NZ - 1)])
+    e_x[x] = jnp.sum(x3[...], axis=0)
     spread("x7", "x", e_x.at[x])
-    stages(2, K // PIVOTS)
+    stages(3, K // PIVOTS)
     inverse = work[:, K:]
     basis[...] = times_transposed(sec[...], inverse) * scale_root
     arrived("y7", e_y.at[pl.ds(0, NZ - 1)])
@@ -464,12 +477,12 @@
         vmem((2, NY, K, BLOCK), bf16), vmem((2, NY, K, BLOCK), bf16),
         vmem((2, NY, 32, BLOCK), bf16), vmem((2, NZ, 64, K), bf16), vmem((2, NX, NY, 16, BLOCK), bf16),
         vmem((2, NY - 1, 32, BLOCK), bf16), vmem((2, NZ - 1, 64, K), bf16), vmem((2, NX - 1, NY, 16, BLOCK), bf16),
-        vmem((2, NZ, 8, K), f32), vmem((2, NY, 8, K), f32), vmem((NY, 16, BLOCK), bf16),
-        vmem((NY, 8, BLOCK), f32), vmem((NZ, 8, BLOCK), f32),
-        vmem((2, NZ - 1, 8, K), f32), vmem((2, NY - 1, 8, K), f32), vmem((NY - 1, 16, BLOCK), bf16),
-        vmem((NY - 1, 8, BLOCK), f32), vmem((NZ - 1, 8, BLOCK), f32),
-        vmem((2, NX, 8, K), f32), vmem((2, NX, 8, K), f32), vmem((NZ, 16, BLOCK), f32),
-        vmem((NZ, 8, BLOCK), f32), vmem((NY, 8, BLOCK), f32),
+        vmem((NY, 8, 3 * K), f32), vmem((NZ, 8, 3 * K), f32), vmem((NY - 1, 8, 3 * K), f32), vmem((NZ - 1, 8, 3 * K), f32),
+        vmem((NZ, 8, K), f32), vmem((NY, 8, K), f32), vmem((NY, 16, BLOCK), bf16),
+        vmem((NZ - 1, 8, K), f32), vmem((NY - 1, 8, K), f32), vmem((NY - 1, 16, BLOCK), bf16),
+        vmem((NX, 8, 2 * K), f32), vmem((NZ, 8, BLOCK), f32), vmem((NY, 8, BLOCK), f32),
+        vmem((NY, 8, 3 * K), f32), vmem((NZ, 8, 3 * K), f32),
+        vmem((NX, 8, K), f32), vmem((NX, 8, K), f32), vmem((NZ, 16, BLOCK), f32),
         vmem((2, NY, NZ, 8, K), f32), vmem((2, NZ, NY, 8, K), f32), vmem((2, NX, 2, NY, 8, BLOCK), f32),
         vmem((NZ, 8, K), f32), vmem((NZ, 8, K), f32), vmem((NX, 16, BLOCK), f32),
         pltpu.SemaphoreType.DMA((2,)), pltpu.SemaphoreType.DMA((16,)), pltpu.SemaphoreType.DMA((8,)),

time: 90 us -> 91.3 us (1.014)
  Pallas kernels: 87 us -> 88.1 us
    pallas_call x1, Pallas kernels: 87 us -> 88.1 us  [on_device(): pl.pallas_call(functools.partial(kernel, math.sqrt(rows_total)), out_shap...]
where the time goes in v4:
time: 91.3 us; the launch traced here: 91 us
  Pallas kernels  88.1 us (96%)
  local copies, waits for them, and re-layouts  2.19 us (2%)
    pallas_call x1, Pallas kernels, on_device(): pl.pallas_call(functools.partial(kernel, math.sqrt(rows_total)), out_shap...  88.1 us
    unnamed x4, local copies, waits for them, and re-layouts  2.19 us

profile of v4, /device:TPU:1, one launch (start us, length us, event | category | flops | bytes accessed | tf_op | source)
XLA Modules:
  0.0 91.0 jit_solution(2309313321222304758)
XLA Ops:
  0.6 0.0 copy-start
  0.6 0.8 copy-done
  1.5 88.1 %subspace.1 = (f32[512,128]{1,0:T(8,128)S(1)}, f32[256,128]{1,0:T(8,128)S(1)}) custom-call(bf16[512,4096]{1,0:T(8,128)(2,1)} %a_hbm.1, bf16[256,128]{1,0:T(8,128)(2,1)S(1)} %copy-done), custom_call_target="tpu_custom_call" | custom-call | tf_op jit(solution)/shard_map/subspace/pallas_call | solution.py:495
  89.6 0.7 copy.6
  90.3 0.7 copy.7
Async XLA Ops:
  0.6 0.8 copy-start

commit v5 on v4

--- a/solution.py
+++ b/solution.py
@@ -232,6 +232,9 @@
                 device_id=partner, device_id_type=pl.DeviceIdType.MESH,
             ).start()
 
+        if p == 0:
+            gram_first()
+
         @pl.loop(0, NY // 2)
         def _(j):
             values = []
@@ -254,8 +257,6 @@
         scatter(f"x1{p}", "x", x1s.at[p], x1r.at[p])
         scatter(f"y1{p}", "y", y1s.at[p], y1r.at[p])
         scatter(f"z1{p}", "z", z1s.at[p], z1r.at[p])
-        if p == 0:
-            gram_first()
 
     def gram_z(p):
         arrived(f"gc{p}", g_col.at[p])

time: 91.3 us -> 88.7 us (0.972)
  Pallas kernels: 88.1 us -> 85.7 us
    pallas_call x1, Pallas kernels: 88.1 us -> 85.7 us  [on_device(): pl.pallas_call(functools.partial(kernel, math.sqrt(rows_total)), out_shap...]
where the time goes in v5:
time: 88.7 us; the launch traced here: 88.6 us
  Pallas kernels  85.7 us (97%)
  local copies, waits for them, and re-layouts  2.19 us (2%)
    pallas_call x1, Pallas kernels, on_device(): pl.pallas_call(functools.partial(kernel, math.sqrt(rows_total)), out_shap...  85.7 us
    unnamed x4, local copies, waits for them, and re-layouts  2.19 us

profile of v5, /device:TPU:1, one launch (start us, length us, event | category | flops | bytes accessed | tf_op | source)
XLA Modules:
  0.0 88.6 jit_solution(5814965771224641117)
XLA Ops:
  0.6 0.0 copy-start
  0.6 0.8 copy-done
  1.5 85.7 %subspace.1 = (f32[512,128]{1,0:T(8,128)S(1)}, f32[256,128]{1,0:T(8,128)S(1)}) custom-call(bf16[512,4096]{1,0:T(8,128)(2,1)} %a_hbm.1, bf16[256,128]{1,0:T(8,128)(2,1)S(1)} %copy-done), custom_call_target="tpu_custom_call" | custom-call | tf_op jit(solution)/shard_map/subspace/pallas_call | solution.py:496
  87.2 0.7 copy.6
  87.9 0.7 copy.7
Async XLA Ops:
  0.6 0.8 copy-start

commit v6 on v5

--- a/solution.py
+++ b/solution.py
@@ -419,8 +419,35 @@
     arrived("x6", f_x.at[other])
     sec[...] = times_transposed(f_acc[...] + second_part(other), work[:, K:])
 
+    def left():
+        for i, ref in pending:
+            pltpu.make_async_copy(ref, ref, send_sems.at[i]).wait()
+        pending.clear()
+
+    def first_left():
+        left()
+        for d in range(NY):
+            pltpu.make_async_copy(mine, mine, s_send.at[8 + d]).wait()
+        for d in NEAR:
+            pltpu.make_async_copy(mine, mine, s_send.at[d]).wait()
+        for d in FAR:
+            quarter = s_v.at[h, y, pl.ds(0, QUARTER)]
+            pltpu.make_async_copy(quarter, quarter, s_send.at[d]).wait()
+            three_quarters = s_v.at[h, y, pl.ds(0, BLOCK - QUARTER)]
+            pltpu.make_async_copy(three_quarters, three_quarters, q_send.at[d]).wait()
+        for p in range(2):
+            for j in range(NY // 2):
+                pair = c_send.at[p, pl.ds(0, 2)]
+                pltpu.make_async_copy(pair, pair, c_sems.at[p, 0, j]).wait()
+        for d in range(1, NY):
+            pltpu.make_async_copy(f_y.at[h, y], f_y.at[h, y], f_sems.at[0, d]).wait()
+            pltpu.make_async_copy(f_z.at[h, z], f_z.at[h, z], f_sems.at[0, 8 + d]).wait()
+        for d in range(1, NX):
+            pltpu.make_async_copy(f_x.at[h, x], f_x.at[h, x], f_sems.at[0, 16 + d]).wait()
+
     project(1, sec[...])
     gram_z(1)
+    first_left()
     gram_x(1)
     two()
     gram_back(1)
@@ -431,6 +458,7 @@
     arrived("z3", z3.at[pl.ds(0, NX - 1)])
     e_z[z] = jnp.sum(z3[...], axis=0)
     spread("z7", "z", e_z.at[z])
+    left()
     gram_done(1)
     stages(0, 3)
     arrived("x3", x3.at[pl.ds(0, NZ - 1)])
@@ -445,26 +473,7 @@
     summed = jnp.concatenate([tiles(e_y), tiles(e_z)] + [e_x[q, k : k + 8] for k in (0, 8) for q in range(NX)], axis=0)
     components[...] = times_transposed(summed.T, inverse) / scale_root
 
-    for i, ref in pending:
-        pltpu.make_async_copy(ref, ref, send_sems.at[i]).wait()
-    for d in range(NY):
-        pltpu.make_async_copy(mine, mine, s_send.at[8 + d]).wait()
-    for d in NEAR:
-        pltpu.make_async_copy(mine, mine, s_send.at[d]).wait()
-    for d in FAR:
-        quarter = s_v.at[h, y, pl.ds(0, QUARTER)]
-        pltpu.make_async_copy(quarter, quarter, s_send.at[d]).wait()
-        three_quarters = s_v.at[h, y, pl.ds(0, BLOCK - QUARTER)]
-        pltpu.make_async_copy(three_quarters, three_quarters, q_send.at[d]).wait()
-    for p in range(2):
-        for j in range(NY // 2):
-            pair = c_send.at[p, pl.ds(0, 2)]
-            pltpu.make_async_copy(pair, pair, c_sems.at[p, 0, j]).wait()
-    for d in range(1, NY):
-        pltpu.make_async_copy(f_y.at[h, y], f_y.at[h, y], f_sems.at[0, d]).wait()
-        pltpu.make_async_copy(f_z.at[h, z], f_z.at[h, z], f_sems.at[0, 8 + d]).wait()
-    for d in range(1, NX):
-        pltpu.make_async_copy(f_x.at[h, x], f_x.at[h, x], f_sems.at[0, 16 + d]).wait()
+    left()
 
 
 def on_device(activations, sketch):

time: 88.7 us -> 88.6 us (level)
  no operation moved by 1% of the time
where the time goes in v6:
time: 88.6 us; the launch traced here: 88.4 us
  Pallas kernels  85.6 us (97%)
  local copies, waits for them, and re-layouts  2.19 us (2%)
    pallas_call x1, Pallas kernels, on_device(): pl.pallas_call(functools.partial(kernel, math.sqrt(rows_total)), out_shap...  85.6 us
    unnamed x4, local copies, waits for them, and re-layouts  2.19 us

profile of v6, /device:TPU:1, one launch (start us, length us, event | category | flops | bytes accessed | tf_op | source)
XLA Modules:
  0.0 88.4 jit_solution(7125305171552631307)
XLA Ops:
  0.6 0.0 copy-start
  0.6 0.8 copy-done
  1.5 85.6 %subspace.1 = (f32[512,128]{1,0:T(8,128)S(1)}, f32[256,128]{1,0:T(8,128)S(1)}) custom-call(bf16[512,4096]{1,0:T(8,128)(2,1)} %a_hbm.1, bf16[256,128]{1,0:T(8,128)(2,1)S(1)} %copy-done), custom_call_target="tpu_custom_call" | custom-call | tf_op jit(solution)/shard_map/subspace/pallas_call | solution.py:505
  87.1 0.7 copy.6
  87.8 0.7 copy.7
Async XLA Ops:
  0.6 0.8 copy-start
